TPU v7x, 512 devices: a whole 4x4x16 slice. The times are simulated.
512 devices in a mesh: ctx: 128 (over y, x, z_lo), tp: 4 (over z_hi, core).
Axes of the slice: x: 4, y: 4, z: 16 (z_hi: 2, z_lo: 8; z = z_hi * 8 + z_lo), core: 2. Of those that a mesh axis runs over, the one named last changes fastest.
Arguments:
- hidden: bfloat16 [32768, 8192], P('ctx', 'tp'), may hold values from -6 to 6
- queries: bfloat16 [32768, 4096], P('ctx', 'tp'), may hold values from -1000 to 1000
- kv_weight: bfloat16 [8192, 1024], P('tp', 'ctx'), may hold values from -0.0625 to 0.0625
- kv_bias: bfloat16 [1024], P('tp'), may hold values from -3 to 3
- window: int32 [4], P('tp'), may hold values from 1024 to 4096, as said below
- segment_ids: int32 [32768], P('ctx'), may hold values from 0 to 15, never falling along the last dimension, each value on 1 to 4096 neighbouring positions
Outputs:
- attended: bfloat16 [32768, 4096], P('ctx', 'tp')
- kv_cache: bfloat16 [32768, 1024], P('ctx', 'tp')
Inputs may be any that keep to these rules, and one draw needn't show every extreme that they name: `window`: each entry is 1024 to 4096; some key head's entry equals 4096.
All inputs are finite; a program needn't handle non-finite values.
Results may differ from a plain program's by a relative error of at most 0.012.
Values may be sent and summed in bfloat16 or wider, within the bound.
No kernel may reach another device: no remote copies, remote signals or barrier semaphores. Data moves between devices by JAX's collectives and lax.ppermute only.
A program may use at most 64 MiB of HBM per device.

v0:
```python
import jax
import jax.numpy as jnp
from jax import lax
from jax.sharding import PartitionSpec as P

WINDOW = 4096
rope_base = 1000000.0


def split_up(array, dim, count):
    dims = array.shape
    tiles = array.reshape(*dims[:dim], count, dims[dim] // count, *dims[dim + 1 :])
    return jnp.moveaxis(tiles, dim, 0)


def sent_and_summed(array, axis, dim):
    count = lax.axis_size(axis)
    tiles = lax.all_to_all(split_up(array, dim, count), axis, 0, 0, tiled=True)
    return jnp.sum(tiles, axis=0)


def passed_along(value, axis, steps):
    count = lax.axis_size(axis)
    initial, last = (max(0, -steps), min(count, count - steps))
    return lax.ppermute(value, axis, [(source, source + steps) for source in range(initial, last)])


def rotate(values, positions):
    half = values.shape[-1] // 2
    freqs = rope_base ** (-2.0 * jnp.arange(half, dtype=jnp.float32) / values.shape[-1])
    angles = positions.astype(jnp.float32)[:, None] * freqs[None, :]
    cosine = jnp.cos(angles)
    sine = jnp.sin(angles)
    former = values[:, :half]
    latter = values[:, half:]
    return jnp.concatenate(
        [former * cosine - latter * sine, latter * cosine + former * sine], axis=1
    )


def attend(carry, query_rows, query_pos, query_seg, reach, block, block_seg, block_pos):
    running_max, running_sum, weighted = carry
    head = block.shape[1] // 2
    scores = lax.dot_general(
        query_rows, block[:, :head], (((1,), (1,)), ((), ())), preferred_element_type=jnp.float32
    )
    scores = scores * head ** (-0.5)
    gap = query_pos[:, None] - block_pos[None, :]
    allowed = (
        (query_seg[:, None] == block_seg[None, :])
        & (gap >= 0)
        & (gap < reach)
        & (block_pos >= 0)[None, :]
    )
    scores = jnp.where(allowed, scores, -jnp.inf)
    newest = jnp.maximum(running_max, jnp.max(scores, axis=1))
    probs = jnp.exp(scores - newest[:, None])
    rescale = jnp.exp(running_max - newest)
    summed = running_sum * rescale + jnp.sum(probs, axis=1)
    mixed = jnp.dot(probs.astype(jnp.bfloat16), block[:, head:], preferred_element_type=jnp.float32)
    return (newest, summed, weighted * rescale[:, None] + mixed)


def body(hidden, queries, kv_weight, kv_bias, window, segment_ids):
    tok_rows = hidden.shape[0]
    terms = jnp.dot(
        hidden,
        lax.all_gather(kv_weight, "ctx", axis=1, tiled=True),
        preferred_element_type=jnp.float32,
    )
    projected = sent_and_summed(terms, "tp", 1)
    projected = projected + kv_bias.astype(jnp.float32)[None, :]
    head = kv_bias.shape[0] // 2
    shard = lax.axis_index("ctx")
    offsets = jnp.arange(tok_rows, dtype=jnp.int32)
    positions = shard * tok_rows + offsets
    cache = jnp.concatenate(
        [rotate(projected[:, :head], positions), projected[:, head:]], axis=1
    ).astype(jnp.bfloat16)
    group = queries.shape[1] // head
    query_rows = queries.reshape(tok_rows * group, head)
    query_pos = jnp.repeat(positions, group)
    query_seg = jnp.repeat(segment_ids, group)
    reach = window[0]

    def absorb(carry, block, block_seg, block_pos):
        return attend(carry, query_rows, query_pos, query_seg, reach, block, block_seg, block_pos)

    row_count = tok_rows * group
    carry = (
        jnp.full((row_count,), -jnp.inf, jnp.float32),
        jnp.zeros((row_count,), jnp.float32),
        jnp.zeros((row_count, head), jnp.float32),
    )
    carry = absorb(carry, cache, segment_ids, positions)
    halo_count = WINDOW // tok_rows
    held_kv = cache
    held_seg = segment_ids
    have = 0
    while have < halo_count:
        got_kv, got_seg = passed_along((held_kv, held_seg), "ctx", max(have, 1))
        shards = got_kv.shape[0] // tok_rows
        for member in range(shards):
            lower = member * tok_rows
            block_pos = (shard - have - shards + member) * tok_rows + offsets
            carry = absorb(
                carry,
                got_kv[lower : lower + tok_rows],
                got_seg[lower : lower + tok_rows],
                block_pos,
            )
        if have == 0:
            held_kv, held_seg = (got_kv, got_seg)
        else:
            held_kv = jnp.concatenate([got_kv, held_kv], axis=0)
            held_seg = jnp.concatenate([got_seg, held_seg], axis=0)
        have = have + shards
    newest, summed, weighted = carry
    attended = (weighted / summed[:, None]).reshape(tok_rows, group * head).astype(jnp.bfloat16)
    return (attended, cache)


def solution(mesh):
    in_specs = (P("ctx", "tp"), P("ctx", "tp"), P("tp", "ctx"), P("tp"), P("tp"), P("ctx"))
    out_specs = (P("ctx", "tp"), P("ctx", "tp"))
    return jax.shard_map(body, mesh=mesh, in_specs=in_specs, out_specs=out_specs, check_vma=False)
```

profile of v0, /device:TPU:2, one launch (start us, length us, event | category | flops | bytes accessed | tf_op | source)
XLA Modules:
  0.0 1188.6 jit_solution(4037237898657685963)
XLA Ops:
  7.2 0.7 all-gather.2.cloned.1.call-update
  7.9 3.8 collective-permute-start
  12.0 937.9 %all-gather.2.cloned.1.call-done = bf16[2048,1024]{0,1:T(8,128)(2,1)} async-done(((bf16[2048,8]{0,1:T(8,128)(2,1)}), bf16[2048,1024]{0,1:T(8,128)(2,1)}) %all-gather.2.cloned.1.call-update) | async-done | bytes 4194320 | tf_op jit(solution)/shard_map/all_gather | solution.py:68
  949.9 3.5 fusion.267
  953.4 1.1 copy.11
  954.5 11.2 all-to-all-start
  965.9 1.9 collective-permute-start.2
  967.8 25.3 %collective-permute-done.2 = s32[256]{0:T(256)S(1)} collective-permute-done((s32[256]{0:T(256)S(1)}, s32[256]{0:T(256)S(1)}, u32[]{:S(2)}, u32[]{:S(2)}) %collective-permute-start.2) | collective-permute-done | bytes 1056 | tf_op jit(solution)/shard_map/ppermute | solution.py:25
  993.1 1.9 collective-permute-start.4
  996.4 9.0 collective-permute-done.4
  1005.4 1.9 collective-permute-start.6
  1007.3 26.5 %collective-permute-done.6 = s32[1024]{0:T(1024)S(1)} collective-permute-done((s32[1024]{0:T(1024)S(1)}, s32[1024]{0:T(1024)S(1)}, u32[]{:S(2)}, u32[]{:S(2)}) %collective-permute-start.6) | collective-permute-done | bytes 4128 | tf_op jit(solution)/shard_map/ppermute | solution.py:25
  1033.8 1.9 collective-permute-start.8
  1035.7 3.6 collective-permute-done.8
  1040.2 4.2 collective-permute-start.1
  1044.4 1.0 fusion.264
  1045.8 8.8 collective-permute-done.1
  1054.5 1.9 collective-permute-start.3
  1056.5 1.0 fusion.265
  1057.5 12.8 %collective-permute-done.3 = bf16[256,256]{1,0:T(8,128)(2,1)S(1)} collective-permute-done((bf16[256,256]{1,0:T(8,128)(2,1)S(1)}, bf16[256,256]{1,0:T(8,128)(2,1)S(1)}, u32[]{:S(2)}, u32[]{:S(2)}) %collective-permute-start.3) | collective-permute-done | bytes 131104 | tf_op jit(solution)/shard_map/ppermute | solution.py:25
  1070.3 1.9 collective-permute-start.5
  1072.2 1.0 fusion.263
  1073.2 19.8 %collective-permute-done.5 = bf16[512,256]{1,0:T(8,128)(2,1)S(1)} collective-permute-done((bf16[512,256]{1,0:T(8,128)(2,1)S(1)}, bf16[512,256]{1,0:T(8,128)(2,1)S(1)}, u32[]{:S(2)}, u32[]{:S(2)}) %collective-permute-start.5) | collective-permute-done | bytes 262176 | tf_op jit(solution)/shard_map/ppermute | solution.py:25
  1093.0 1.9 collective-permute-start.7
  1095.0 1.0 fusion.261
  1096.0 1.0 fusion.262
  1097.0 29.6 %collective-permute-done.7 = bf16[1024,256]{1,0:T(8,128)(2,1)S(1)} collective-permute-done((bf16[1024,256]{1,0:T(8,128)(2,1)S(1)}, bf16[1024,256]{1,0:T(8,128)(2,1)S(1)}, u32[]{:S(2)}, u32[]{:S(2)}) %collective-permute-start.7) | collective-permute-done | bytes 524320 | tf_op jit(solution)/shard_map/ppermute | solution.py:25
  1126.7 2.2 collective-permute-start.9
  1128.9 1.0 fusion.257
  1129.9 1.0 fusion.258
  1130.9 1.0 fusion.259
  1131.9 1.0 fusion.260
  1132.9 20.8 %collective-permute-done.9 = bf16[2048,256]{1,0:T(8,128)(2,1)S(1)} collective-permute-done((bf16[2048,256]{1,0:T(8,128)(2,1)S(1)}, bf16[2048,256]{1,0:T(8,128)(2,1)S(1)}, u32[]{:S(2)}, u32[]{:S(2)}) %collective-permute-start.9) | collective-permute-done | bytes 1048608 | tf_op jit(solution)/shard_map/ppermute | solution.py:25
  1153.7 1.0 fusion.249
  1154.6 1.0 fusion.250
  1155.6 1.0 fusion.251
  1156.6 1.0 fusion.252
  1157.6 1.0 fusion.253
  1158.6 1.0 fusion.254
  1159.6 1.0 fusion.255
  1160.6 1.0 fusion.256
  1161.6 0.8 fusion.147
  1163.0 0.6 fusion.139
  1164.2 0.6 fusion.131
  1166.6 0.9 fusion.40
  1175.0 0.7 fusion.39
  1175.7 5.1 fusion.63
  1180.8 1.0 convert_element_type.88
  (93 shorter events, 12.7 us)
Async XLA Ops:
  7.2 942.7 %copy-start = (bf16[256,2048]{1,0:T(8,128)(2,1)S(1)}, bf16[256,2048]{1,0:T(8,128)(2,1)}, u32[]{:S(2)}) copy-start(bf16[256,2048]{1,0:T(8,128)(2,1)} %param.6) | copy-start | bytes 3145732
  7.2 942.7 %all-gather.2.cloned.1.call-start = ((), (), s32[]{:S(2)}) async-start(), calls=%async_computation.1 | async-start | bytes 4227072 | tf_op jit(solution)/shard_map/all_gather | solution.py:68
  7.9 957.9 %collective-permute-start = (s32[256]{0:T(256)}, s32[256]{0:T(256)S(1)}, u32[]{:S(2)}, u32[]{:S(2)}) collective-permute-start(s32[256]{0:T(256)} %param.11), channel_id=1, source_target_pairs={{0,4},{4,8},{8,12},{12,16},{16,20},{20,24},{24,28},{28,32},{32,36}... | collective-permute-start | bytes 3080 | tf_op jit(solution)/shard_map/ppermute | solution.py:25
  953.3 42.3 %copy-start.5 = (bf16[256]{0:T(256)(128)(2,1)S(1)}, bf16[256]{0:T(256)(128)(2,1)}, u32[]{:S(2)}) copy-start(bf16[256]{0:T(256)(128)(2,1)} %param.9) | copy-start | bytes 1540
  953.4 42.6 %copy-start.4 = (s32[256]{0:T(256)S(1)}, s32[256]{0:T(256)}, u32[]{:S(2)}) copy-start(s32[256]{0:T(256)} %param.11) | copy-start | bytes 3076
  953.4 42.8 %copy-start.2 = (bf16[256,1024]{1,0:T(8,128)(2,1)S(1)}, bf16[256,1024]{1,0:T(8,128)(2,1)}, u32[]{:S(2)}) copy-start(bf16[256,1024]{1,0:T(8,128)(2,1)} %param.7) | copy-start | bytes 1572868
  954.5 84.9 %all-to-all-start = ((f32[4,256,256]{2,1,0:T(8,128)}), f32[4,256,256]{2,1,0:T(8,128)S(1)}, u32[]{:S(2)}, u32[]{:S(2)}) async-start(f32[4,256,256]{2,1,0:T(8,128)} %bitcast.94), calls=%async_computation | async-start | bytes 2097152 | tf_op jit(solution)/shard_map/all_to_all | solution.py:18
  965.9 27.2 %collective-permute-start.2 = (s32[256]{0:T(256)S(1)}, s32[256]{0:T(256)S(1)}, u32[]{:S(2)}, u32[]{:S(2)}) collective-permute-start(s32[256]{0:T(256)S(1)} %collective-permute-done), channel_id=1, source_target_pairs={{0,4},{4,8},{8,12},{12,16},{16,20},{20,24},{24,28},{28,32},{32,36}... | collective-permute-start | bytes 3080 | tf_op jit(solution)/shard_map/ppermute | solution.py:25
  993.1 12.3 %collective-permute-start.4 = (s32[512]{0:T(512)S(1)}, s32[512]{0:T(512)S(1)}, u32[]{:S(2)}, u32[]{:S(2)}) collective-permute-start(s32[512]{0:T(512)S(1)} %pad_add_fusion.2), channel_id=1, source_target_pairs={{0,8},{4,12},{8,16},{12,20},{16,24},{20,28},{24,32},{28,36},{32,40... | collective-permute-start | bytes 6152 | tf_op jit(solution)/shard_map/ppermute | solution.py:25
  1005.4 28.4 %collective-permute-start.6 = (s32[1024]{0:T(1024)S(1)}, s32[1024]{0:T(1024)S(1)}, u32[]{:S(2)}, u32[]{:S(2)}) collective-permute-start(s32[1024]{0:T(1024)S(1)} %pad_add_fusion.1), channel_id=1, source_target_pairs={{0,16},{4,20},{8,24},{12,28},{16,32},{20,36},{24,40},{28,44},{32,4... | collective-permute-start | bytes 12296 | tf_op jit(solution)/shard_map/ppermute | solution.py:25
  1033.8 5.5 collective-permute-start.8
  1040.2 5.3 copy-start.3
  1040.2 14.4 %collective-permute-start.1 = (bf16[256,256]{1,0:T(8,128)(2,1)S(1)}, bf16[256,256]{1,0:T(8,128)(2,1)S(1)}, u32[]{:S(2)}, u32[]{:S(2)}) collective-permute-start(bf16[256,256]{1,0:T(8,128)(2,1)S(1)} %pad_maximum_fusion.3), channel_id=1, source_target_pairs={{0,4},{4,8},{8,12},{12,16},{16,20},{20,24},{24,28},{28,32},{32,36}... | collective-permute-start | bytes 393224 | tf_op jit(solution)/shard_map/ppermute | solution.py:25
  1054.5 15.7 %collective-permute-start.3 = (bf16[256,256]{1,0:T(8,128)(2,1)S(1)}, bf16[256,256]{1,0:T(8,128)(2,1)S(1)}, u32[]{:S(2)}, u32[]{:S(2)}) collective-permute-start(bf16[256,256]{1,0:T(8,128)(2,1)S(1)} %collective-permute-done.1), channel_id=1, source_target_pairs={{0,4},{4,8},{8,12},{12,16},{16,20},{20,24},{24,28},{28,32},{32,36}... | collective-permute-start | bytes 393224 | tf_op jit(solution)/shard_map/ppermute | solution.py:25
  1070.3 22.7 %collective-permute-start.5 = (bf16[512,256]{1,0:T(8,128)(2,1)S(1)}, bf16[512,256]{1,0:T(8,128)(2,1)S(1)}, u32[]{:S(2)}, u32[]{:S(2)}) collective-permute-start(bf16[512,256]{1,0:T(8,128)(2,1)S(1)} %pad_maximum_fusion.2), channel_id=1, source_target_pairs={{0,8},{4,12},{8,16},{12,20},{16,24},{20,28},{24,32},{28,36},{32,40... | collective-permute-start | bytes 786440 | tf_op jit(solution)/shard_map/ppermute | solution.py:25
  1093.0 33.6 %collective-permute-start.7 = (bf16[1024,256]{1,0:T(8,128)(2,1)S(1)}, bf16[1024,256]{1,0:T(8,128)(2,1)S(1)}, u32[]{:S(2)}, u32[]{:S(2)}) collective-permute-start(bf16[1024,256]{1,0:T(8,128)(2,1)S(1)} %pad_maximum_fusion.1), channel_id=1, source_target_pairs={{0,16},{4,20},{8,24},{12,28},{16,32},{20,36},{24,40},{28,44},{32,4... | collective-permute-start | bytes 1572872 | tf_op jit(solution)/shard_map/ppermute | solution.py:25
  1126.7 27.0 %collective-permute-start.9 = (bf16[2048,256]{1,0:T(8,128)(2,1)S(1)}, bf16[2048,256]{1,0:T(8,128)(2,1)S(1)}, u32[]{:S(2)}, u32[]{:S(2)}) collective-permute-start(bf16[2048,256]{1,0:T(8,128)(2,1)S(1)} %pad_maximum_fusion), channel_id=1, source_target_pairs={{0,32},{4,36},{8,40},{12,44},{16,48},{20,52},{24,56},{28,60},{32,6... | collective-permute-start | bytes 3145736 | tf_op jit(solution)/shard_map/ppermute | solution.py:25
  1175.7 6.1 copy-start.1
Sparse Core Ops, SparseCore 0:
  10.1 939.7 all-gather.1
where the time goes:
time: 1190 us
  waiting for transfers between devices  1090 us (92%)
  starting transfers between devices  34.9 us (3%)
  matrix products  34.4 us (3%)
  between operations  15.4 us (1%)
    all_gather x1, waiting for transfers between devices, body(): lax.all_gather(kv_weight, 'ctx', axis=1, tiled=True)  938 us
    ppermute x10, waiting for transfers between devices, passed_along(): lax.ppermute(value, axis, [(source, source + steps) for source in range(i...  156 us
  transfers between devices with their start and end apart: 12, of which 10 were waited for; matrix products, arithmetic and copies ran while one was open for 1% of the time, Pallas kernels for 0%

commit v1 on v0

--- a/solution.py
+++ b/solution.py
@@ -65,7 +65,9 @@
     tok_rows = hidden.shape[0]
     terms = jnp.dot(
         hidden,
-        lax.all_gather(kv_weight, "ctx", axis=1, tiled=True),
+        jnp.concatenate(
+            lax.all_to_all(jnp.stack([kv_weight] * lax.axis_size("ctx")), "ctx", 0, 0), axis=1
+        ),
         preferred_element_type=jnp.float32,
     )
     projected = sent_and_summed(terms, "tp", 1)

time: 1190 us -> 461 us (0.39)
  the two profiles are of different devices: /device:TPU:2 before, /device:TPU:24 now
where the time goes in v1:
time: 461 us; the launch traced here: 453 us
  waiting for transfers between devices  352 us (76%)
  starting transfers between devices  51.2 us (11%)
  matrix products  35.3 us (8%)
  other arithmetic  6.43 us (1%)
  local copies, waits for them, and re-layouts  5.04 us (1%)
    all_to_all x1, waiting for transfers between devices, body(): lax.all_to_all(jnp.stack([kv_weight] * lax.axis_size('ctx')), 'ctx', 0, 0)  183 us
    ppermute x10, waiting for transfers between devices, passed_along(): lax.ppermute(value, axis, [(source, source + steps) for source in range(i...  169 us
    ppermute x10, starting transfers between devices, passed_along(): lax.ppermute(value, axis, [(source, source + steps) for source in range(i...  23.2 us
    all_to_all x1, starting transfers between devices, body(): lax.all_to_all(jnp.stack([kv_weight] * lax.axis_size('ctx')), 'ctx', 0, 0)  20.3 us
    dot_general x17, matrix products, attend(): lax.dot_general(query_rows, block[:, :head], (((1,), (1,)), ((), ())), pr...  16.8 us
    dot_general x17, matrix products, attend(): jnp.dot(probs.astype(jnp.bfloat16), block[:, head:], preferred_element_ty...  14.1 us
  transfers between devices with their start and end apart: 12, of which 10 were waited for; matrix products, arithmetic and copies ran while one was open for 3% of the time, Pallas kernels for 0%

profile of v1, /device:TPU:24, one launch (start us, length us, event | category | flops | bytes accessed | tf_op | source)
XLA Modules:
  0.0 452.8 jit_solution(2584476795503524130)
XLA Ops:
  0.6 3.3 stack.2
  4.0 20.3 %all-to-all-start = ((bf16[128,2048,8]{1,2,0:T(8,128)(2,1)}), bf16[128,2048,8]{1,2,0:T(8,128)(2,1)}, u32[]{:S(2)}, u32[]{:S(2)}) async-start(bf16[128,2048,8]{1,2,0:T(8,128)(2,1)} %stack.2), calls=%async_computation | async-start | bytes 8388608 | tf_op jit(solution)/shard_map/all_to_all | solution.py:69
  24.3 3.4 collective-permute-start
  27.9 183.0 %all-to-all-done = bf16[128,2048,8]{1,2,0:T(8,128)(2,1)} async-done(((bf16[128,2048,8]{1,2,0:T(8,128)(2,1)}), bf16[128,2048,8]{1,2,0:T(8,128)(2,1)}, u32[]{:S(2)}, u32[]{:S(2)}) %all-to-all-start) | async-done | bytes 4194336 | tf_op jit(solution)/shard_map/all_to_all | solution.py:69
  210.9 4.4 convolution_bitcast_fusion
  215.4 7.7 %all-to-all-start.1 = ((f32[4,256,256]{2,1,0:T(8,128)}), f32[4,256,256]{2,1,0:T(8,128)S(1)}, u32[]{:S(2)}, u32[]{:S(2)}) async-start(f32[4,256,256]{2,1,0:T(8,128)} %convolution_bitcast_fusion), calls=%async_computation.1 | async-start | bytes 2097152 | tf_op jit(solution)/shard_map/all_to_all | solution.py:18
  223.3 1.9 collective-permute-start.2
  225.2 44.1 %collective-permute-done.2 = s32[256]{0:T(256)S(1)} collective-permute-done((s32[256]{0:T(256)S(1)}, s32[256]{0:T(256)S(1)}, u32[]{:S(2)}, u32[]{:S(2)}) %collective-permute-start.2) | collective-permute-done | bytes 1056 | tf_op jit(solution)/shard_map/ppermute | solution.py:25
  269.3 1.9 collective-permute-start.4
  272.6 10.9 %collective-permute-done.4 = s32[512]{0:T(512)S(1)} collective-permute-done((s32[512]{0:T(512)S(1)}, s32[512]{0:T(512)S(1)}, u32[]{:S(2)}, u32[]{:S(2)}) %collective-permute-start.4) | collective-permute-done | bytes 2080 | tf_op jit(solution)/shard_map/ppermute | solution.py:25
  283.5 1.9 collective-permute-start.6
  285.5 10.5 %collective-permute-done.6 = s32[1024]{0:T(1024)S(1)} collective-permute-done((s32[1024]{0:T(1024)S(1)}, s32[1024]{0:T(1024)S(1)}, u32[]{:S(2)}, u32[]{:S(2)}) %collective-permute-start.6) | collective-permute-done | bytes 4128 | tf_op jit(solution)/shard_map/ppermute | solution.py:25
  295.9 1.9 collective-permute-start.8
  297.9 5.7 %collective-permute-done.8 = s32[2048]{0:T(1024)S(1)} collective-permute-done((s32[2048]{0:T(1024)S(1)}, s32[2048]{0:T(1024)S(1)}, u32[]{:S(2)}, u32[]{:S(2)}) %collective-permute-start.8) | collective-permute-done | bytes 8224 | tf_op jit(solution)/shard_map/ppermute | solution.py:25
  304.4 4.3 collective-permute-start.1
  308.7 1.0 fusion.265
  310.1 10.8 %collective-permute-done.1 = bf16[256,256]{1,0:T(8,128)(2,1)S(1)} collective-permute-done((bf16[256,256]{1,0:T(8,128)(2,1)S(1)}, bf16[256,256]{1,0:T(8,128)(2,1)S(1)}, u32[]{:S(2)}, u32[]{:S(2)}) %collective-permute-start.1) | collective-permute-done | bytes 131104 | tf_op jit(solution)/shard_map/ppermute | solution.py:25
  320.9 1.9 collective-permute-start.3
  322.8 1.0 fusion.266
  323.8 15.0 %collective-permute-done.3 = bf16[256,256]{1,0:T(8,128)(2,1)S(1)} collective-permute-done((bf16[256,256]{1,0:T(8,128)(2,1)S(1)}, bf16[256,256]{1,0:T(8,128)(2,1)S(1)}, u32[]{:S(2)}, u32[]{:S(2)}) %collective-permute-start.3) | collective-permute-done | bytes 131104 | tf_op jit(solution)/shard_map/ppermute | solution.py:25
  338.8 1.9 collective-permute-start.5
  340.7 1.0 fusion.264
  341.7 19.8 %collective-permute-done.5 = bf16[512,256]{1,0:T(8,128)(2,1)S(1)} collective-permute-done((bf16[512,256]{1,0:T(8,128)(2,1)S(1)}, bf16[512,256]{1,0:T(8,128)(2,1)S(1)}, u32[]{:S(2)}, u32[]{:S(2)}) %collective-permute-start.5) | collective-permute-done | bytes 262176 | tf_op jit(solution)/shard_map/ppermute | solution.py:25
  361.6 1.9 collective-permute-start.7
  363.5 1.0 fusion.262
  364.5 1.0 fusion.263
  365.5 29.6 %collective-permute-done.7 = bf16[1024,256]{1,0:T(8,128)(2,1)S(1)} collective-permute-done((bf16[1024,256]{1,0:T(8,128)(2,1)S(1)}, bf16[1024,256]{1,0:T(8,128)(2,1)S(1)}, u32[]{:S(2)}, u32[]{:S(2)}) %collective-permute-start.7) | collective-permute-done | bytes 524320 | tf_op jit(solution)/shard_map/ppermute | solution.py:25
  395.2 2.1 collective-permute-start.9
  397.3 1.0 fusion.258
  398.3 1.0 fusion.259
  399.3 1.0 fusion.260
  400.3 1.0 fusion.261
  401.3 23.0 %collective-permute-done.9 = bf16[2048,256]{1,0:T(8,128)(2,1)S(1)} collective-permute-done((bf16[2048,256]{1,0:T(8,128)(2,1)S(1)}, bf16[2048,256]{1,0:T(8,128)(2,1)S(1)}, u32[]{:S(2)}, u32[]{:S(2)}) %collective-permute-start.9) | collective-permute-done | bytes 1048608 | tf_op jit(solution)/shard_map/ppermute | solution.py:25
  424.3 1.0 fusion.250
  425.3 1.0 fusion.251
  426.3 1.0 fusion.252
  427.3 1.0 fusion.253
  428.3 1.0 fusion.254
  429.3 1.0 fusion.255
  430.3 1.0 fusion.256
  431.3 1.0 fusion.257
  432.3 0.8 fusion.147
  433.7 0.6 fusion.139
  434.3 0.6 fusion.135
  437.3 0.9 fusion.40
  445.7 0.7 fusion.39
  446.4 5.0 %fusion.63 = bf16[2048,128]{1,0:T(8,128)(2,1)S(1)} fusion(f32[2048,128]{1,0:T(8,128)S(1)} %fusion.151, f32[2048,128]{1,0:T(8,128)S(1)} %fusion.153, f32[2048,128]{1,0:T(8,128)S(1)} %fusion.155, f32[2048,128]{1,0:T(8,128)S(1)} %fusion.157, f32[2048,128]{1,0:T(8,128)S(1)} %fusion.159, f32[2048,128]{1,0:T(8,128)S(1)} %fusion.161, ...), kind=kOutput, calls=%fused_computation.117 | convolution fusion | flops 143392768 | bytes 18546688 | tf_op jit(solution)/shard_map/dot_general | solution.py:60
  451.4 1.0 convert_element_type.88
  (92 shorter events, 12.6 us)
Async XLA Ops:
  0.6 210.3 %copy-start = (bf16[256,2048]{1,0:T(8,128)(2,1)S(1)}, bf16[256,2048]{1,0:T(8,128)(2,1)}, u32[]{:S(2)}) copy-start(bf16[256,2048]{1,0:T(8,128)(2,1)} %param.6) | copy-start | bytes 3145732
  4.0 20.3 %copy-start.4 = (s32[256]{0:T(256)S(1)}, s32[256]{0:T(256)}, u32[]{:S(2)}) copy-start(s32[256]{0:T(256)} %param.11) | copy-start | bytes 3076
  4.0 207.0 %all-to-all-start = ((bf16[128,2048,8]{1,2,0:T(8,128)(2,1)}), bf16[128,2048,8]{1,2,0:T(8,128)(2,1)}, u32[]{:S(2)}, u32[]{:S(2)}) async-start(bf16[128,2048,8]{1,2,0:T(8,128)(2,1)} %stack.2), calls=%async_computation | async-start | bytes 8388608 | tf_op jit(solution)/shard_map/all_to_all | solution.py:69
  24.3 199.0 %collective-permute-start = (s32[256]{0:T(256)S(1)}, s32[256]{0:T(256)S(1)}, u32[]{:S(2)}, u32[]{:S(2)}) collective-permute-start(s32[256]{0:T(256)S(1)} %copy-done.4), channel_id=1, source_target_pairs={{0,4},{4,8},{8,12},{12,16},{16,20},{20,24},{24,28},{28,32},{32,36}... | collective-permute-start | bytes 3080 | tf_op jit(solution)/shard_map/ppermute | solution.py:25
  215.4 56.5 %copy-start.5 = (bf16[256]{0:T(256)(128)(2,1)S(1)}, bf16[256]{0:T(256)(128)(2,1)}, u32[]{:S(2)}) copy-start(bf16[256]{0:T(256)(128)(2,1)} %param.9) | copy-start | bytes 1540
  215.4 57.0 %copy-start.2 = (bf16[256,1024]{1,0:T(8,128)(2,1)S(1)}, bf16[256,1024]{1,0:T(8,128)(2,1)}, u32[]{:S(2)}) copy-start(bf16[256,1024]{1,0:T(8,128)(2,1)} %param.7) | copy-start | bytes 1572868
  215.4 88.2 %all-to-all-start.1 = ((f32[4,256,256]{2,1,0:T(8,128)}), f32[4,256,256]{2,1,0:T(8,128)S(1)}, u32[]{:S(2)}, u32[]{:S(2)}) async-start(f32[4,256,256]{2,1,0:T(8,128)} %convolution_bitcast_fusion), calls=%async_computation.1 | async-start | bytes 2097152 | tf_op jit(solution)/shard_map/all_to_all | solution.py:18
  223.3 46.0 %collective-permute-start.2 = (s32[256]{0:T(256)S(1)}, s32[256]{0:T(256)S(1)}, u32[]{:S(2)}, u32[]{:S(2)}) collective-permute-start(s32[256]{0:T(256)S(1)} %collective-permute-done), channel_id=1, source_target_pairs={{0,4},{4,8},{8,12},{12,16},{16,20},{20,24},{24,28},{28,32},{32,36}... | collective-permute-start | bytes 3080 | tf_op jit(solution)/shard_map/ppermute | solution.py:25
  269.3 14.2 %collective-permute-start.4 = (s32[512]{0:T(512)S(1)}, s32[512]{0:T(512)S(1)}, u32[]{:S(2)}, u32[]{:S(2)}) collective-permute-start(s32[512]{0:T(512)S(1)} %pad_add_fusion.2), channel_id=1, source_target_pairs={{0,8},{4,12},{8,16},{12,20},{16,24},{20,28},{24,32},{28,36},{32,40... | collective-permute-start | bytes 6152 | tf_op jit(solution)/shard_map/ppermute | solution.py:25
  283.5 12.4 %collective-permute-start.6 = (s32[1024]{0:T(1024)S(1)}, s32[1024]{0:T(1024)S(1)}, u32[]{:S(2)}, u32[]{:S(2)}) collective-permute-start(s32[1024]{0:T(1024)S(1)} %pad_add_fusion.1), channel_id=1, source_target_pairs={{0,16},{4,20},{8,24},{12,28},{16,32},{20,36},{24,40},{28,44},{32,4... | collective-permute-start | bytes 12296 | tf_op jit(solution)/shard_map/ppermute | solution.py:25
  295.9 7.6 %collective-permute-start.8 = (s32[2048]{0:T(1024)S(1)}, s32[2048]{0:T(1024)S(1)}, u32[]{:S(2)}, u32[]{:S(2)}) collective-permute-start(s32[2048]{0:T(1024)S(1)} %pad_add_fusion), channel_id=1, source_target_pairs={{0,32},{4,36},{8,40},{12,44},{16,48},{20,52},{24,56},{28,60},{32,6... | collective-permute-start | bytes 24584 | tf_op jit(solution)/shard_map/ppermute | solution.py:25
  304.4 5.3 %copy-start.3 = (bf16[256,256]{1,0:T(8,128)(2,1)}, bf16[256,256]{1,0:T(8,128)(2,1)S(1)}, u32[]{:S(2)}) copy-start(bf16[256,256]{1,0:T(8,128)(2,1)S(1)} %pad_maximum_fusion.3) | copy-start | bytes 393220
  304.4 16.5 %collective-permute-start.1 = (bf16[256,256]{1,0:T(8,128)(2,1)S(1)}, bf16[256,256]{1,0:T(8,128)(2,1)S(1)}, u32[]{:S(2)}, u32[]{:S(2)}) collective-permute-start(bf16[256,256]{1,0:T(8,128)(2,1)S(1)} %pad_maximum_fusion.3), channel_id=1, source_target_pairs={{0,4},{4,8},{8,12},{12,16},{16,20},{20,24},{24,28},{28,32},{32,36}... | collective-permute-start | bytes 393224 | tf_op jit(solution)/shard_map/ppermute | solution.py:25
  320.9 17.9 %collective-permute-start.3 = (bf16[256,256]{1,0:T(8,128)(2,1)S(1)}, bf16[256,256]{1,0:T(8,128)(2,1)S(1)}, u32[]{:S(2)}, u32[]{:S(2)}) collective-permute-start(bf16[256,256]{1,0:T(8,128)(2,1)S(1)} %collective-permute-done.1), channel_id=1, source_target_pairs={{0,4},{4,8},{8,12},{12,16},{16,20},{20,24},{24,28},{28,32},{32,36}... | collective-permute-start | bytes 393224 | tf_op jit(solution)/shard_map/ppermute | solution.py:25
  338.8 22.7 %collective-permute-start.5 = (bf16[512,256]{1,0:T(8,128)(2,1)S(1)}, bf16[512,256]{1,0:T(8,128)(2,1)S(1)}, u32[]{:S(2)}, u32[]{:S(2)}) collective-permute-start(bf16[512,256]{1,0:T(8,128)(2,1)S(1)} %pad_maximum_fusion.2), channel_id=1, source_target_pairs={{0,8},{4,12},{8,16},{12,20},{16,24},{20,28},{24,32},{28,36},{32,40... | collective-permute-start | bytes 786440 | tf_op jit(solution)/shard_map/ppermute | solution.py:25
  361.6 33.6 %collective-permute-start.7 = (bf16[1024,256]{1,0:T(8,128)(2,1)S(1)}, bf16[1024,256]{1,0:T(8,128)(2,1)S(1)}, u32[]{:S(2)}, u32[]{:S(2)}) collective-permute-start(bf16[1024,256]{1,0:T(8,128)(2,1)S(1)} %pad_maximum_fusion.1), channel_id=1, source_target_pairs={{0,16},{4,20},{8,24},{12,28},{16,32},{20,36},{24,40},{28,44},{32,4... | collective-permute-start | bytes 1572872 | tf_op jit(solution)/shard_map/ppermute | solution.py:25
  395.2 29.1 %collective-permute-start.9 = (bf16[2048,256]{1,0:T(8,128)(2,1)S(1)}, bf16[2048,256]{1,0:T(8,128)(2,1)S(1)}, u32[]{:S(2)}, u32[]{:S(2)}) collective-permute-start(bf16[2048,256]{1,0:T(8,128)(2,1)S(1)} %pad_maximum_fusion), channel_id=1, source_target_pairs={{0,32},{4,36},{8,40},{12,44},{16,48},{20,52},{24,56},{28,60},{32,6... | collective-permute-start | bytes 3145736 | tf_op jit(solution)/shard_map/ppermute | solution.py:25
  446.4 6.1 %copy-start.1 = (bf16[256,2048]{1,0:T(8,128)(2,1)S(1)}, bf16[256,2048]{1,0:T(8,128)(2,1)}, u32[]{:S(2)}) copy-start(bf16[256,2048]{1,0:T(8,128)(2,1)} %param.6) | copy-start | bytes 3145732
